TPU v7x, 32 devices: a whole 2x2x4 slice. The times are simulated.
32 devices in a mesh: dp: 8 (over y, x, core), fsdp: 4 (over z).
Axes of the slice: x: 2, y: 2, z: 4, core: 2. Of those that a mesh axis runs over, the one named last changes fastest.
Arguments:
- queries: bfloat16 [8192, 2048], P(('dp', 'fsdp')), may hold values from -600 to 600
- w_kv: bfloat16 [2, 2048, 896], P(None, 'fsdp'), may hold values from -0.1875 to 0.1875
- encodings: bfloat16 [12288, 896], P(('dp', 'fsdp')), may hold values from -6 to 6
- counts: int32 [32], P(('dp', 'fsdp')), may hold values from 48 to 384, as said below
- owner_rank: int32 [12288], P(('dp', 'fsdp')), may hold values from 0 to 7, as said below
- owner_span: int32 [12288], P(('dp', 'fsdp')), may hold values from 0 to 3, as said below
- grad_ctx: bfloat16 [8192, 2048], P(('dp', 'fsdp')), may hold values from -6 to 6
Outputs:
- grad_queries: bfloat16 [8192, 2048], P(('dp', 'fsdp'))
- grad_value: bfloat16 [2048, 896], P('fsdp')
Inputs may be any that keep to these rules, and one draw needn't show every extreme that they name: `counts`: each count is 384 divided by 1, 2, 4 or 8; among the devices of equal fsdp index one holds 384. `owner_rank`: among the live rows of one device at most 48 name the same owner; a device whose count is 384 names every owner exactly 48 times. `owner_span`: every span of every decoder device is named by at least one live row of a device with equal fsdp index.
All inputs are finite; a program needn't handle non-finite values.
Results may differ from a plain program's by a relative error of at most 0.023.
Values may be sent and summed in bfloat16 or wider, within the bound.
A program may use at most 64 MiB of HBM per device.

v0:
```python
import jax
import jax.numpy as jnp
from jax import lax
from jax.sharding import PartitionSpec as P

HEADS = 16
HEAD_DIM = 128
SPAN = 64


def pack_rows(enc_rows, live_count, rank_rows, span_rows, dp_count):
    row_total = enc_rows.shape[0]
    pair_slots = row_total // dp_count
    live_rows = jnp.arange(row_total, dtype=jnp.int32) < live_count
    hit_table = (
        (rank_rows[:, None] == jnp.arange(dp_count, dtype=jnp.int32)[None, :]) & live_rows[:, None]
    ).astype(jnp.int32)
    before_hits = jnp.cumsum(hit_table, axis=0) - hit_table
    slot_index = jnp.sum(before_hits * hit_table, axis=1)
    target = jnp.where(live_rows, rank_rows * pair_slots + slot_index, dp_count * pair_slots)
    buffer = (
        jnp.zeros((dp_count * pair_slots, enc_rows.shape[1]), enc_rows.dtype)
        .at[target]
        .set(enc_rows, mode="drop")
    )
    tag_buffer = (
        jnp.full((dp_count * pair_slots,), -1, jnp.int32).at[target].set(span_rows, mode="drop")
    )
    return (
        buffer.reshape(dp_count, pair_slots, enc_rows.shape[1]),
        tag_buffer.reshape(dp_count, pair_slots),
    )


def local(queries, w_kv, encodings, counts, owner_rank, owner_span, grad_ctx):
    dp_count = lax.axis_size("dp")
    slot_total = encodings.shape[0]
    width = encodings.shape[1]
    buffer, tag_buffer = pack_rows(encodings, counts[0], owner_rank, owner_span, dp_count)
    arrived, arrived_tags = (
        lax.all_to_all(buffer, "dp", split_axis=0, concat_axis=0, tiled=True),
        lax.all_to_all(tag_buffer, "dp", split_axis=0, concat_axis=0, tiled=True),
    )
    received = arrived.reshape(slot_total, width)
    tag_rows = arrived_tags.reshape(slot_total)
    contract = (((1,), (1,)), ((), ()))

    def project_one(piece):
        return lax.dot_general(
            received, piece, contract, preferred_element_type=jnp.float32
        ).astype(jnp.bfloat16)

    keys = project_one(lax.all_gather(w_kv[0], "fsdp", axis=0, tiled=True))
    values = project_one(lax.all_gather(w_kv[1], "fsdp", axis=0, tiled=True))
    token_total = queries.shape[0]
    scale = 1.0 / HEAD_DIM**0.5
    query_heads = queries.reshape(token_total, HEADS, HEAD_DIM)
    key_heads = keys.reshape(slot_total, HEADS, HEAD_DIM)
    value_heads = values.reshape(slot_total, HEADS, HEAD_DIM)
    grad_heads = grad_ctx.reshape(token_total, HEADS, HEAD_DIM)
    scores = (
        jnp.einsum("thd,khd->htk", query_heads, key_heads, preferred_element_type=jnp.float32)
        * scale
    )
    token_span = jnp.arange(token_total, dtype=jnp.int32) // SPAN
    allowed = (token_span[:, None] == tag_rows[None, :])[None]
    masked = jnp.where(allowed, scores, -1e30)
    highest = jnp.max(masked, axis=-1, keepdims=True)
    weights = jnp.where(allowed, jnp.exp(masked - highest), 0.0)
    probs = weights / jnp.sum(weights, axis=-1, keepdims=True)
    probs_low = probs.astype(jnp.bfloat16)
    context = jnp.einsum("htk,khd->thd", probs_low, value_heads, preferred_element_type=jnp.float32)
    dprob = jnp.einsum("thd,khd->htk", grad_heads, value_heads, preferred_element_type=jnp.float32)
    delta = jnp.transpose(jnp.sum(grad_heads.astype(jnp.float32) * context, axis=-1))[:, :, None]
    dscore = (probs * (dprob - delta)).astype(jnp.bfloat16)
    grad_query = (
        jnp.einsum("htk,khd->thd", dscore, key_heads, preferred_element_type=jnp.float32) * scale
    )
    grad_queries = grad_query.astype(jnp.bfloat16).reshape(token_total, HEADS * HEAD_DIM)
    dval = jnp.einsum("htk,thd->khd", probs_low, grad_heads, preferred_element_type=jnp.float32)
    dval = dval.astype(jnp.bfloat16).reshape(slot_total, HEADS * HEAD_DIM)
    piece = dval
    shard_sum = lax.psum_scatter(
        lax.dot_general(
            piece, received, (((0,), (0,)), ((), ())), preferred_element_type=jnp.float32
        ).astype(jnp.bfloat16),
        "fsdp",
        scatter_dimension=0,
        tiled=True,
    )
    group_sum = lax.psum(shard_sum, "dp").astype(jnp.float32)
    grad_value = (group_sum / dp_count).astype(jnp.bfloat16)
    return (grad_queries, grad_value)


def solution(mesh):
    in_specs = (
        P(("dp", "fsdp"), None),
        P(None, "fsdp", None),
        P(("dp", "fsdp"), None),
        P(("dp", "fsdp")),
        P(("dp", "fsdp")),
        P(("dp", "fsdp")),
        P(("dp", "fsdp"), None),
    )
    out_specs = (P(("dp", "fsdp"), None), P("fsdp", None))
    return jax.shard_map(local, mesh=mesh, in_specs=in_specs, out_specs=out_specs, check_vma=False)
```

profile of v0, /device:TPU:0, one launch (start us, length us, event | category | flops | bytes accessed | tf_op | source)
XLA Modules:
  0.0 295.7 jit_solution(8508736633667711385)
XLA Ops:
  7.2 0.0 copy-start
  7.2 0.0 copy-start.5
  7.2 0.0 copy-start.4
  7.2 0.0 all-gather.5.cloned.1.call-start
  7.2 3.0 %fusion.39 = (bf16[1,512,896]{2,1,0:T(8,128)(2,1)}, bf16[1,512,896]{2,1,0:T(8,128)(2,1)}) fusion(bf16[2,512,896]{2,1,0:T(8,128)(2,1)} %param.8), kind=kLoop, calls=%fused_computation.54 | loop fusion | bytes 3670016 | tf_op jit(solution)/shard_map/slice | solution.py:54
  10.2 0.0 all-gather.5.cloned.1.call-update
  10.2 0.0 all-gather.7.cloned.1.call-start
  10.3 0.7 all-gather.7.cloned.1.call-update
  11.6 0.0 copy-done.5
  11.7 0.9 reduce-window.6
  12.5 0.2 slice_reduce_fusion
  12.8 0.1 fusion.31
  12.9 3.1 %scatter_custom_fusion.1 = s32[384]{0:T(512)S(1)} fusion(s32[384]{0:T(512)S(1)} %compare_select_fusion, s32[384]{0:T(512)} %param.12, s32[]{:T(128)} %constant.40.clone.1), kind=kCustom, calls=%fused_computation.50 | custom fusion | bytes 2048 | tf_op jit(solution)/shard_map/scatter | solution.py:27
  16.0 0.7 all_to_all.10
  16.7 5.2 %all-to-all-start.1 = ((s32[8,1,48]{2,1,0:T(1,128)}), s32[8,1,48]{2,1,0:T(1,128)S(1)}, u32[]{:S(2)}, u32[]{:S(2)}) async-start(s32[8,1,48]{2,1,0:T(1,128)} %all_to_all.10), calls=%async_computation.1 | async-start | bytes 8192 | tf_op jit(solution)/shard_map/all_to_all | solution.py:42
  21.8 3.7 %scatter_custom_fusion = bf16[384,896]{1,0:T(8,128)(2,1)} fusion(s32[384]{0:T(512)S(1)} %compare_select_fusion, bf16[384,896]{1,0:T(8,128)(2,1)} %param.9, bf16[]{:T(256)} %constant.16.clone.1), kind=kCustom, calls=%fused_computation.31 | custom fusion | bytes 688640 | tf_op jit(solution)/shard_map/scatter | solution.py:24
  25.5 0.9 all-to-all-done.1
  26.4 3.5 %all-to-all-start = ((bf16[8,48,896]{2,1,0:T(8,128)(2,1)}), bf16[8,48,896]{2,1,0:T(8,128)(2,1)S(1)}, u32[]{:S(2)}, u32[]{:S(2)}) async-start(bf16[8,48,896]{2,1,0:T(8,128)(2,1)} %bitcast.4), calls=%async_computation | async-start | bytes 1376256 | tf_op jit(solution)/shard_map/all_to_all | solution.py:41
  30.0 0.2 reduce-scatter.2.cloned.1.call-start
  30.2 1.3 copy.25
  31.5 0.6 broadcast.95
  32.1 0.7 reduce.5
  32.8 0.1 eq.50
  32.9 0.1 broadcast_compare_fusion
  33.0 8.4 %all-to-all-done = bf16[8,48,896]{2,1,0:T(8,128)(2,1)S(1)} async-done(((bf16[8,48,896]{2,1,0:T(8,128)(2,1)}), bf16[8,48,896]{2,1,0:T(8,128)(2,1)S(1)}, u32[]{:S(2)}, u32[]{:S(2)}) %all-to-all-start) | async-done | bytes 688160 | tf_op jit(solution)/shard_map/all_to_all | solution.py:41
  41.4 43.8 %all-gather.5.cloned.1.call-done = bf16[1,2048,896]{2,1,0:T(8,128)(2,1)} async-done(((bf16[1,512,896]{2,1,0:T(8,128)(2,1)}), bf16[1,2048,896]{2,1,0:T(8,128)(2,1)}) %all-gather.5.cloned.1.call-update) | async-done | bytes 3670032 | tf_op jit(solution)/shard_map/all_gather | solution.py:53
  85.2 5.0 %fusion.15 = bf16[384,2048]{1,0:T(8,128)(2,1)} fusion(bf16[384,896]{1,0:T(8,128)(2,1)S(1)} %bitcast.87, bf16[1,2048,896]{2,1,0:T(8,128)(2,1)} %all-gather.5.cloned.1.call-done), kind=kOutput, calls=%fused_computation.20 | convolution fusion | flops 1410072576 | bytes 5931008 | tf_op jit(solution)/shard_map/dot_general | solution.py:49
  90.2 1.9 copy.42
  92.1 1.0 fusion.25
  93.2 2.5 fusion.40
  95.7 0.0 copy-start.3
  95.7 0.7 fusion.21
  96.4 1.9 copy-done.2
  98.3 1.6 copy-done.1
  100.0 1.0 convolution_convert_fusion.1
  101.0 4.1 %convolution_convert_fusion = bf16[2048,896]{1,0:T(8,128)(2,1)} fusion(bf16[384,2048]{0,1:T(8,128)(2,1)S(1)} %bitcast.85, bf16[384,896]{1,0:T(8,128)(2,1)S(1)} %bitcast.88), kind=kOutput, calls=%fused_computation.12 | convolution fusion | flops 1411121152 | bytes 5931008 | tf_op jit(solution)/shard_map/dot_general | solution.py:84
  105.1 0.0 reduce-scatter.2.cloned.1.call-update
  105.1 0.3 all-reduce.2.cloned.1.call-start
  105.4 52.7 %all-gather.7.cloned.1.call-done = bf16[1,2048,896]{2,1,0:T(8,128)(2,1)} async-done(((bf16[1,512,896]{2,1,0:T(8,128)(2,1)}), bf16[1,2048,896]{2,1,0:T(8,128)(2,1)}) %all-gather.7.cloned.1.call-update) | async-done | bytes 3670032 | tf_op jit(solution)/shard_map/all_gather | solution.py:54
  158.1 5.0 %fusion.18 = bf16[384,2048]{1,0:T(8,128)(2,1)} fusion(bf16[384,896]{1,0:T(8,128)(2,1)S(1)} %bitcast.89, bf16[1,2048,896]{2,1,0:T(8,128)(2,1)} %all-gather.7.cloned.1.call-done), kind=kOutput, calls=%fused_computation.21 | convolution fusion | flops 1410072576 | bytes 5931008 | tf_op jit(solution)/shard_map/dot_general | solution.py:49
  163.1 2.6 copy.43
  165.7 3.4 %fusion.22 = f32[256,16]{0,1:T(8,128)S(1)} fusion(bf16[256,16,128]{0,2,1:T(8,128)(2,1)} %bitcast.80, bf16[384,16,128]{0,2,1:T(8,128)(2,1)} %bitcast.83, bf16[16,256,384]{1,2,0:T(8,128)(2,1)} %copy-done.1), kind=kOutput, calls=%fused_computation.24 | convolution fusion | flops 404221952 | bytes 5783552 | tf_op jit(solution)/shard_map/htk,khd->thd/dot_general | solution.py:72
  169.1 58.4 %reduce-scatter.2.cloned.1.call-done = bf16[512,896]{1,0:T(8,128)(2,1)} async-done(((bf16[2048,896]{1,0:T(8,128)(2,1)}), bf16[512,896]{1,0:T(8,128)(2,1)}) %reduce-scatter.2.cloned.1.call-update) | async-done | bytes 917520 | tf_op jit(solution)/shard_map/reduce_scatter | solution.py:83
  227.5 0.0 all-reduce.2.cloned.1.call-update
  227.5 6.6 %multiply_convert_fusion = bf16[16,128,256]{2,1,0:T(8,128)(2,1)} fusion(bf16[384,16,128]{0,2,1:T(8,128)(2,1)S(1)} %bitcast.79, f32[16,256]{1,0:T(8,128)S(1)} %bitcast.92, bf16[384,16,128]{0,2,1:T(8,128)(2,1)} %bitcast.84, bf16[256,16,128]{0,2,1:T(8,128)(2,1)} %bitcast.81, f32[16,256,384]{1,2,0:T(8,128)} %copy-done.2, f32[16,256]{1,0:T(8,128)S(1)} %get-tuple-element.10), kind=kOutput, calls=%fused_computation.25 | convolution fusion | flops 812646400 | bytes 11567104 | tf_op jit(solution)/shard_map/htk,khd->thd/dot_general | solution.py:77
  234.1 2.3 copy.35
  236.3 50.6 %all-reduce.2.cloned.1.call-done = bf16[512,896]{1,0:T(8,128)(2,1)} async-done(((bf16[512,896]{1,0:T(8,128)(2,1)}), bf16[512,896]{1,0:T(8,128)(2,1)}) %all-reduce.2.cloned.1.call-update) | async-done | bytes 917520 | tf_op jit(solution)/shard_map/psum | solution.py:91
  286.9 2.3 multiply_convert_fusion.1
  (11 shorter events, 0.1 us)
Async XLA Ops:
  7.2 85.0 %copy-start = (bf16[256,2048]{1,0:T(8,128)(2,1)S(1)}, bf16[256,2048]{1,0:T(8,128)(2,1)}, u32[]{:S(2)}) copy-start(bf16[256,2048]{1,0:T(8,128)(2,1)} %param.7) | copy-start | bytes 3145732
  7.2 4.5 %copy-start.5 = (s32[384]{0:T(512)S(1)}, s32[384]{0:T(512)}, u32[]{:S(2)}) copy-start(s32[384]{0:T(512)} %param.11) | copy-start | bytes 4612
  7.2 23.0 %copy-start.4 = (bf16[256,2048]{1,0:T(8,128)(2,1)S(1)}, bf16[256,2048]{1,0:T(8,128)(2,1)}, u32[]{:S(2)}) copy-start(bf16[256,2048]{1,0:T(8,128)(2,1)} %param.13) | copy-start | bytes 3145732
  7.2 78.0 %all-gather.5.cloned.1.call-start = ((), (), s32[]{:S(2)}) async-start(), calls=%async_computation.5 | async-start | bytes 4587520 | tf_op jit(solution)/shard_map/all_gather | solution.py:53
  10.2 147.9 %all-gather.7.cloned.1.call-start = ((), (), s32[]{:S(2)}) async-start(), calls=%async_computation.6 | async-start | bytes 4587520 | tf_op jit(solution)/shard_map/all_gather | solution.py:54
  16.7 9.8 %all-to-all-start.1 = ((s32[8,1,48]{2,1,0:T(1,128)}), s32[8,1,48]{2,1,0:T(1,128)S(1)}, u32[]{:S(2)}, u32[]{:S(2)}) async-start(s32[8,1,48]{2,1,0:T(1,128)} %all_to_all.10), calls=%async_computation.1 | async-start | bytes 8192 | tf_op jit(solution)/shard_map/all_to_all | solution.py:42
  26.4 15.0 %all-to-all-start = ((bf16[8,48,896]{2,1,0:T(8,128)(2,1)}), bf16[8,48,896]{2,1,0:T(8,128)(2,1)S(1)}, u32[]{:S(2)}, u32[]{:S(2)}) async-start(bf16[8,48,896]{2,1,0:T(8,128)(2,1)} %bitcast.4), calls=%async_computation | async-start | bytes 1376256 | tf_op jit(solution)/shard_map/all_to_all | solution.py:41
  30.0 197.5 %reduce-scatter.2.cloned.1.call-start = ((), (), s32[]{:S(2)}) async-start(), calls=%async_computation.3 | async-start | bytes 4587520 | tf_op jit(solution)/shard_map/reduce_scatter | solution.py:83
  95.7 2.7 copy-start.2
  95.7 4.3 %copy-start.3 = (bf16[256,2048]{0,1:T(8,128)(2,1)S(1)}, bf16[256,2048]{0,1:T(8,128)(2,1)}, u32[]{:S(2)}) copy-start(bf16[256,2048]{0,1:T(8,128)(2,1)} %copy.25) | copy-start | bytes 3145732
  98.3 1.6 copy-start.1
  105.1 181.8 %all-reduce.2.cloned.1.call-start = ((), (), s32[]{:S(2)}) async-start(), calls=%async_computation.4 | async-start | bytes 1835008 | tf_op jit(solution)/shard_map/psum | solution.py:91
Sparse Core Ops, SparseCore 0:
  10.4 74.7 all-gather.4
  87.3 70.7 all-gather.6
  160.4 67.0 reduce-scatter.1
  230.5 56.3 all-reduce.1
where the time goes:
time: 296 us
  waiting for transfers between devices  215 us (73%)
  matrix products  26.1 us (9%)
  local copies, waits for them, and re-layouts  22.8 us (8%)
  between operations  14.6 us (5%)
  starting transfers between devices  9.28 us (3%)
  other arithmetic  7.35 us (2%)
    reduce_scatter x1, waiting for transfers between devices, local(): lax.psum_scatter(lax.dot_general(piece, received, (((0,), (0,)), ((), ())...  58.4 us
    all_gather x1, waiting for transfers between devices, local(): values = project_one(lax.all_gather(w_kv[1], 'fsdp', axis=0, tiled=True))  52.7 us
    psum x1, waiting for transfers between devices, local(): group_sum = lax.psum(shard_sum, 'dp').astype(jnp.float32)  50.6 us
    all_gather x1, waiting for transfers between devices, local(): keys = project_one(lax.all_gather(w_kv[0], 'fsdp', axis=0, tiled=True))  43.8 us
    dot_general x2, matrix products, project_one(): lax.dot_general(received, piece, contract, preferred_element_type=jnp.flo...  10.1 us
    all_to_all x1, waiting for transfers between devices, local(): lax.all_to_all(buffer, 'dp', split_axis=0, concat_axis=0, tiled=True)  8.36 us
    unnamed x14, local copies, waits for them, and re-layouts  7.15 us
    dot_general x1, matrix products, local(): jnp.einsum('htk,khd->thd', dscore, key_heads, preferred_element_type=jnp....  6.58 us
  transfers between devices with their start and end apart: 6, of which 6 were waited for; matrix products, arithmetic and copies ran while one was open for 16% of the time, Pallas kernels for 0%

commit v1 on v0

--- a/solution.py
+++ b/solution.py
@@ -11,21 +11,18 @@
 def pack_rows(enc_rows, live_count, rank_rows, span_rows, dp_count):
     row_total = enc_rows.shape[0]
     pair_slots = row_total // dp_count
-    live_rows = jnp.arange(row_total, dtype=jnp.int32) < live_count
-    hit_table = (
-        (rank_rows[:, None] == jnp.arange(dp_count, dtype=jnp.int32)[None, :]) & live_rows[:, None]
-    ).astype(jnp.int32)
-    before_hits = jnp.cumsum(hit_table, axis=0) - hit_table
-    slot_index = jnp.sum(before_hits * hit_table, axis=1)
-    target = jnp.where(live_rows, rank_rows * pair_slots + slot_index, dp_count * pair_slots)
-    buffer = (
-        jnp.zeros((dp_count * pair_slots, enc_rows.shape[1]), enc_rows.dtype)
-        .at[target]
-        .set(enc_rows, mode="drop")
-    )
-    tag_buffer = (
-        jnp.full((dp_count * pair_slots,), -1, jnp.int32).at[target].set(span_rows, mode="drop")
-    )
+    rows = jnp.arange(row_total, dtype=jnp.int32)
+    live_rows = rows < live_count
+    hits = (rank_rows[:, None] == jnp.arange(dp_count, dtype=jnp.int32)[None, :]) & live_rows[:, None]
+    earlier = (rows[None, :] < rows[:, None]).astype(jnp.bfloat16)
+    before = jnp.dot(earlier, hits.astype(jnp.bfloat16), preferred_element_type=jnp.float32)
+    slot_index = jnp.sum(jnp.where(hits, before, 0.0), axis=1).astype(jnp.int32)
+    target = jnp.where(live_rows, rank_rows * pair_slots + slot_index, -1)
+    placed = target[None, :] == rows[:, None]
+    buffer = jnp.dot(
+        placed.astype(jnp.bfloat16), enc_rows, preferred_element_type=jnp.float32
+    ).astype(jnp.bfloat16)
+    tag_buffer = jnp.sum(jnp.where(placed, span_rows[None, :] + 1, 0), axis=1) - 1
     return (
         buffer.reshape(dp_count, pair_slots, enc_rows.shape[1]),
         tag_buffer.reshape(dp_count, pair_slots),

time: 296 us -> 296 us (level)
  local copies, waits for them, and re-layouts: 22.8 us -> 15.8 us
  waiting for transfers between devices: 215 us -> 222 us
    scatter x2 -> x0, local copies, waits for them, and re-layouts: 6.73 us -> none  [the longest x1 3.65 us: pack_rows(): buffer = jnp.zeros((dp_count * pair_slots, enc_rows.shape[1]), enc_rows.d...]
    all_gather x1, waiting for transfers between devices: 43.8 us -> 47.7 us  [local(): keys = project_one(lax.all_gather(w_kv[0], 'fsdp', axis=0, tiled=True))]
    unnamed x14 -> x18, local copies, waits for them, and re-layouts: 7.15 us -> 7.12 us
  transfers between devices with their start and end apart: 6 -> 6, of which waited for: 6 -> 6; matrix products, arithmetic and copies ran while one was open for 16% -> 14% of each run, Pallas kernels for 0% -> 0%
where the time goes in v1:
time: 296 us
  waiting for transfers between devices  222 us (75%)
  matrix products  27.7 us (9%)
  local copies, waits for them, and re-layouts  15.8 us (5%)
  between operations  14.6 us (5%)
  starting transfers between devices  9.06 us (3%)
  other arithmetic  6.37 us (2%)
    reduce_scatter x1, waiting for transfers between devices, local(): lax.psum_scatter(lax.dot_general(piece, received, (((0,), (0,)), ((), ())...  58.4 us
    all_gather x1, waiting for transfers between devices, local(): values = project_one(lax.all_gather(w_kv[1], 'fsdp', axis=0, tiled=True))  52.8 us
    psum x1, waiting for transfers between devices, local(): group_sum = lax.psum(shard_sum, 'dp').astype(jnp.float32)  50.6 us
    all_gather x1, waiting for transfers between devices, local(): keys = project_one(lax.all_gather(w_kv[0], 'fsdp', axis=0, tiled=True))  47.7 us
    dot_general x2, matrix products, project_one(): lax.dot_general(received, piece, contract, preferred_element_type=jnp.flo...  10 us
    all_to_all x1, waiting for transfers between devices, local(): lax.all_to_all(buffer, 'dp', split_axis=0, concat_axis=0, tiled=True)  8.73 us
    unnamed x18, local copies, waits for them, and re-layouts  7.12 us
    dot_general x1, matrix products, local(): jnp.einsum('htk,khd->thd', dscore, key_heads, preferred_element_type=jnp....  6.57 us
  transfers between devices with their start and end apart: 6, of which 6 were waited for; matrix products, arithmetic and copies ran while one was open for 14% of the time, Pallas kernels for 0%

profile of v1, /device:TPU:0, one launch (start us, length us, event | category | flops | bytes accessed | tf_op | source)
XLA Modules:
  0.0 295.7 jit_solution(16780972609382700915)
XLA Ops:
  7.2 0.0 copy-start
  7.2 0.0 copy-start.6
  7.2 0.0 copy-start.7
  7.2 0.0 all-gather.5.cloned.1.call-start
  7.3 2.9 fusion.36
  10.2 0.0 all-gather.5.cloned.1.call-update
  10.2 0.0 all-gather.7.cloned.1.call-start
  10.3 0.7 all-gather.7.cloned.1.call-update
  11.6 0.2 fusion.25
  11.8 0.0 copy-done.7
  11.9 0.1 select_reduce_fusion
  12.0 0.7 sub.33
  12.7 5.2 %all-to-all-start.1 = ((s32[8,1,48]{2,1,0:T(1,128)}), s32[8,1,48]{2,1,0:T(1,128)S(1)}, u32[]{:S(2)}, u32[]{:S(2)}) async-start(s32[8,1,48]{2,1,0:T(1,128)} %sub.33), calls=%async_computation.1 | async-start | bytes 8192 | tf_op jit(solution)/shard_map/all_to_all | solution.py:39
  17.9 1.4 convolution_convert_fusion.2
  19.3 3.2 %all-to-all-done.1 = s32[8,1,48]{2,1,0:T(1,128)S(1)} async-done(((s32[8,1,48]{2,1,0:T(1,128)}), s32[8,1,48]{2,1,0:T(1,128)S(1)}, u32[]{:S(2)}, u32[]{:S(2)}) %all-to-all-start.1) | async-done | bytes 1568 | tf_op jit(solution)/shard_map/all_to_all | solution.py:39
  22.5 3.5 %all-to-all-start = ((bf16[8,48,896]{2,1,0:T(8,128)(2,1)}), bf16[8,48,896]{2,1,0:T(8,128)(2,1)S(1)}, u32[]{:S(2)}, u32[]{:S(2)}) async-start(bf16[8,48,896]{2,1,0:T(8,128)(2,1)} %bitcast.1), calls=%async_computation | async-start | bytes 1376256 | tf_op jit(solution)/shard_map/all_to_all | solution.py:38
  26.0 0.0 reduce-scatter.2.cloned.1.call-start
  26.1 0.0 copy-done.4
  26.1 1.3 copy.26
  27.4 0.5 broadcast.82
  27.9 0.6 reduce.3
  28.5 0.1 eq.49
  28.6 0.1 broadcast_compare_fusion
  28.7 8.7 %all-to-all-done = bf16[8,48,896]{2,1,0:T(8,128)(2,1)S(1)} async-done(((bf16[8,48,896]{2,1,0:T(8,128)(2,1)}), bf16[8,48,896]{2,1,0:T(8,128)(2,1)S(1)}, u32[]{:S(2)}, u32[]{:S(2)}) %all-to-all-start) | async-done | bytes 688160 | tf_op jit(solution)/shard_map/all_to_all | solution.py:38
  37.4 47.7 %all-gather.5.cloned.1.call-done = bf16[1,2048,896]{2,1,0:T(8,128)(2,1)} async-done(((bf16[1,512,896]{2,1,0:T(8,128)(2,1)}), bf16[1,2048,896]{2,1,0:T(8,128)(2,1)}) %all-gather.5.cloned.1.call-update) | async-done | bytes 3670032 | tf_op jit(solution)/shard_map/all_gather | solution.py:50
  85.2 5.0 %fusion.15 = bf16[384,2048]{1,0:T(8,128)(2,1)} fusion(bf16[384,896]{1,0:T(8,128)(2,1)S(1)} %bitcast.77, bf16[1,2048,896]{2,1,0:T(8,128)(2,1)} %all-gather.5.cloned.1.call-done), kind=kOutput, calls=%fused_computation.18 | convolution fusion | flops 1410072576 | bytes 5931008 | tf_op jit(solution)/shard_map/dot_general | solution.py:46
  90.2 1.9 copy.43
  92.1 1.0 fusion.26
  93.1 2.5 fusion.37
  95.7 0.0 copy-start.3
  95.7 0.7 fusion.21
  96.4 1.9 copy-done.2
  98.3 1.6 copy-done.1
  99.9 0.0 copy-done.3
  99.9 1.0 convolution_convert_fusion.1
  100.9 4.1 %convolution_convert_fusion = bf16[2048,896]{1,0:T(8,128)(2,1)} fusion(bf16[384,2048]{0,1:T(8,128)(2,1)S(1)} %bitcast.75, bf16[384,896]{1,0:T(8,128)(2,1)S(1)} %bitcast.78), kind=kOutput, calls=%fused_computation.10 | convolution fusion | flops 1411121152 | bytes 5931008 | tf_op jit(solution)/shard_map/dot_general | solution.py:81
  105.0 0.0 reduce-scatter.2.cloned.1.call-update
  105.1 0.2 all-reduce.2.cloned.1.call-start
  105.3 52.8 %all-gather.7.cloned.1.call-done = bf16[1,2048,896]{2,1,0:T(8,128)(2,1)} async-done(((bf16[1,512,896]{2,1,0:T(8,128)(2,1)}), bf16[1,2048,896]{2,1,0:T(8,128)(2,1)}) %all-gather.7.cloned.1.call-update) | async-done | bytes 3670032 | tf_op jit(solution)/shard_map/all_gather | solution.py:51
  158.1 5.0 %fusion.18 = bf16[384,2048]{1,0:T(8,128)(2,1)} fusion(bf16[384,896]{1,0:T(8,128)(2,1)S(1)} %bitcast.79, bf16[1,2048,896]{2,1,0:T(8,128)(2,1)} %all-gather.7.cloned.1.call-done), kind=kOutput, calls=%fused_computation.19 | convolution fusion | flops 1410072576 | bytes 5931008 | tf_op jit(solution)/shard_map/dot_general | solution.py:46
  163.1 2.6 copy.44
  165.7 3.4 %fusion.22 = f32[256,16]{0,1:T(8,128)S(1)} fusion(bf16[256,16,128]{0,2,1:T(8,128)(2,1)} %bitcast.70, bf16[384,16,128]{0,2,1:T(8,128)(2,1)} %bitcast.73, bf16[16,256,384]{1,2,0:T(8,128)(2,1)} %copy-done.1), kind=kOutput, calls=%fused_computation.22 | convolution fusion | flops 404221952 | bytes 5783552 | tf_op jit(solution)/shard_map/htk,khd->thd/dot_general | solution.py:69
  169.1 58.4 %reduce-scatter.2.cloned.1.call-done = bf16[512,896]{1,0:T(8,128)(2,1)} async-done(((bf16[2048,896]{1,0:T(8,128)(2,1)}), bf16[512,896]{1,0:T(8,128)(2,1)}) %reduce-scatter.2.cloned.1.call-update) | async-done | bytes 917520 | tf_op jit(solution)/shard_map/reduce_scatter | solution.py:80
  227.4 0.0 all-reduce.2.cloned.1.call-update
  227.5 6.6 %multiply_convert_fusion = bf16[16,128,256]{2,1,0:T(8,128)(2,1)} fusion(bf16[384,16,128]{0,2,1:T(8,128)(2,1)S(1)} %bitcast.69, f32[16,256]{1,0:T(8,128)S(1)} %bitcast.80, bf16[384,16,128]{0,2,1:T(8,128)(2,1)} %bitcast.74, bf16[256,16,128]{0,2,1:T(8,128)(2,1)} %bitcast.71, f32[16,256,384]{1,2,0:T(8,128)} %copy-done.2, f32[16,256]{1,0:T(8,128)S(1)} %get-tuple-element.10), kind=kOutput, calls=%fused_computation.23 | convolution fusion | flops 812646400 | bytes 11567104 | tf_op jit(solution)/shard_map/htk,khd->thd/dot_general | solution.py:74
  234.0 2.3 copy.36
  236.3 50.6 %all-reduce.2.cloned.1.call-done = bf16[512,896]{1,0:T(8,128)(2,1)} async-done(((bf16[512,896]{1,0:T(8,128)(2,1)}), bf16[512,896]{1,0:T(8,128)(2,1)}) %all-reduce.2.cloned.1.call-update) | async-done | bytes 917520 | tf_op jit(solution)/shard_map/psum | solution.py:88
  286.9 2.3 multiply_convert_fusion.1
  (11 shorter events, 0.0 us)
Async XLA Ops:
  7.2 84.9 %copy-start = (bf16[256,2048]{1,0:T(8,128)(2,1)S(1)}, bf16[256,2048]{1,0:T(8,128)(2,1)}, u32[]{:S(2)}) copy-start(bf16[256,2048]{1,0:T(8,128)(2,1)} %param.7) | copy-start | bytes 3145732
  7.2 4.4 %copy-start.6 = (s32[384]{0:T(512)S(1)}, s32[384]{0:T(512)}, u32[]{:S(2)}) copy-start(s32[384]{0:T(512)} %param.11) | copy-start | bytes 4612
  7.2 4.6 %copy-start.7 = (s32[384]{0:T(512)S(1)}, s32[384]{0:T(512)}, u32[]{:S(2)}) copy-start(s32[384]{0:T(512)} %param.12) | copy-start | bytes 4612
  7.2 10.7 %copy-start.5 = (bf16[384,896]{1,0:T(8,128)(2,1)S(1)}, bf16[384,896]{1,0:T(8,128)(2,1)}, u32[]{:S(2)}) copy-start(bf16[384,896]{1,0:T(8,128)(2,1)} %param.9) | copy-start | bytes 2064388
  7.2 78.0 %all-gather.5.cloned.1.call-start = ((), (), s32[]{:S(2)}) async-start(), calls=%async_computation.5 | async-start | bytes 4587520 | tf_op jit(solution)/shard_map/all_gather | solution.py:50
  10.2 15.9 %copy-start.4 = (bf16[256,2048]{1,0:T(8,128)(2,1)S(1)}, bf16[256,2048]{1,0:T(8,128)(2,1)}, u32[]{:S(2)}) copy-start(bf16[256,2048]{1,0:T(8,128)(2,1)} %param.13) | copy-start | bytes 3145732
  10.2 147.9 %all-gather.7.cloned.1.call-start = ((), (), s32[]{:S(2)}) async-start(), calls=%async_computation.6 | async-start | bytes 4587520 | tf_op jit(solution)/shard_map/all_gather | solution.py:51
  12.7 9.8 %all-to-all-start.1 = ((s32[8,1,48]{2,1,0:T(1,128)}), s32[8,1,48]{2,1,0:T(1,128)S(1)}, u32[]{:S(2)}, u32[]{:S(2)}) async-start(s32[8,1,48]{2,1,0:T(1,128)} %sub.33), calls=%async_computation.1 | async-start | bytes 8192 | tf_op jit(solution)/shard_map/all_to_all | solution.py:39
  22.5 15.0 %all-to-all-start = ((bf16[8,48,896]{2,1,0:T(8,128)(2,1)}), bf16[8,48,896]{2,1,0:T(8,128)(2,1)S(1)}, u32[]{:S(2)}, u32[]{:S(2)}) async-start(bf16[8,48,896]{2,1,0:T(8,128)(2,1)} %bitcast.1), calls=%async_computation | async-start | bytes 1376256 | tf_op jit(solution)/shard_map/all_to_all | solution.py:38
  26.0 201.4 %reduce-scatter.2.cloned.1.call-start = ((), (), s32[]{:S(2)}) async-start(), calls=%async_computation.3 | async-start | bytes 4587520 | tf_op jit(solution)/shard_map/reduce_scatter | solution.py:80
  95.6 2.6 copy-start.2
  95.7 4.3 %copy-start.3 = (bf16[256,2048]{0,1:T(8,128)(2,1)S(1)}, bf16[256,2048]{0,1:T(8,128)(2,1)}, u32[]{:S(2)}) copy-start(bf16[256,2048]{0,1:T(8,128)(2,1)} %copy.26) | copy-start | bytes 3145732
  98.3 1.6 copy-start.1
  105.1 181.8 %all-reduce.2.cloned.1.call-start = ((), (), s32[]{:S(2)}) async-start(), calls=%async_computation.4 | async-start | bytes 1835008 | tf_op jit(solution)/shard_map/psum | solution.py:88
Sparse Core Ops, SparseCore 0:
  10.3 74.8 all-gather.4
  87.3 70.6 all-gather.6
  160.4 67.0 reduce-scatter.1
  230.5 56.3 all-reduce.1
